TPU v7x, 32 devices: a whole 2x2x4 slice. The times are simulated.
32 devices in a mesh: slab: 8 (over z, y), thick: 4 (over x, core).
Axes of the slice: x: 2, y: 2, z: 4, core: 2. Of those that a mesh axis runs over, the one named last changes fastest.
Arguments:
- ref_pos: float32 [3, 524288], P(None, ('slab', 'thick')), may hold values from 0 to 8
- displacement: float32 [3, 524288], P(None, ('slab', 'thick')), may hold values from -1 to 1
- weighted_volume: float32 [524288], P(('slab', 'thick')), may hold values from 10 to 100
- ghost_corner_lists: int32 [2, 2, 512], P(None, None, ('slab', 'thick')), may hold values from 0 to 127
- bond_row_tiles: int32 [4096], P(('slab', 'thick')), may hold values from 0 to 127
- bond_column_tiles: int32 [4096], P(('slab', 'thick')), may hold values from 0 to 319, as said below
- bond_count: int32 [32], P(('slab', 'thick')), may hold values from 32 to 128, as said below
- bond_masks: int32 [4096, 16, 128], P(('slab', 'thick')), may hold values from 0 to 255
- broken_bonds: int32 [4096, 16, 128], P(('slab', 'thick')), may hold values from 0 to 255
Outputs:
- force: float32 [3, 524288], P(None, ('slab', 'thick'))
- dilatation: float32 [524288], P(('slab', 'thick'))
Inputs may be any that keep to these rules, and one draw needn't show every extreme that they name: `bond_column_tiles`: an entry c below 128 names an owned tile; an entry at or above it names cycle cell (c - 128) // 16, only of neighbours that exist. `bond_count`: some device has exactly 128 live slots in every draw; live slots come first.
All inputs are finite; a program needn't handle non-finite values.
Results may differ from a plain program's by a relative error of at most 0.00015.
Values sent between devices are 32-bit elements; how exact they have to be, the bound alone decides.
A program may use at most 64 MiB of HBM per device.

v0:
```python
import jax
import jax.numpy as jnp
from jax import lax
from jax.sharding import PartitionSpec as P

young = 25.0
poisson = 0.22
bulk_modulus = young / (3.0 * (1.0 - 2.0 * poisson))
shear_modulus = young / (2.0 * (1.0 + poisson))
volumetric_term = 3.0 * bulk_modulus - 5.0 * shear_modulus
shear_term = 15.0 * shear_modulus
radius_floor = 0.5
cycle_cells = (0, 1, 2, 3, 4, 7, 8, 11, 12, 13, 14, 15)
highest = lax.Precision.HIGHEST


def extended(block, sides, width):
    for axis, dim in sides:
        count = lax.axis_size(axis)
        forward = [(i, i + 1) for i in range(count - 1)]
        backward = [(target, source) for source, target in forward]
        low = lax.ppermute(
            lax.slice_in_dim(block, block.shape[dim] - width, None, axis=dim), axis, forward
        )
        high = lax.ppermute(lax.slice_in_dim(block, 0, width, axis=dim), axis, backward)
        block = jnp.concatenate([low, block, high], axis=dim)
    return block


def unpack_words(packed):
    shifts = jnp.arange(8, dtype=jnp.int32)
    spread = jnp.right_shift(packed[:, :, None, :], shifts[None, None, :, None]) & 1
    return spread.reshape(packed.shape[0], 128, 128).astype(jnp.float32)


def bond_geometry(
    row_payload,
    column_payload,
    packed_mask_words,
    fractured_bit_words,
    own_tile_list,
    active_slot_flags,
):
    ref_vec = column_payload[0:3, :, None, :] - row_payload[0:3, :, :, None]
    cur_vec = ref_vec + (column_payload[3:6, :, None, :] - row_payload[3:6, :, :, None])
    ref_len = jnp.maximum(jnp.sqrt(jnp.sum(ref_vec * ref_vec, axis=0)), radius_floor)
    cur_len = jnp.maximum(jnp.sqrt(jnp.sum(cur_vec * cur_vec, axis=0)), radius_floor)
    stretch = cur_len - ref_len
    below_diag = jnp.arange(128)[:, None] < jnp.arange(128)[None, :]
    keep_pair = (
        jnp.where(own_tile_list[:, None, None], below_diag[None], True)
        & active_slot_flags[:, None, None]
    )
    unbroken_flags = (
        unpack_words(packed_mask_words)
        * (1.0 - unpack_words(fractured_bit_words))
        * keep_pair.astype(jnp.float32)
    )
    return (unbroken_flags, ref_len, cur_len, stretch, cur_vec)


def stretch_terms(
    row_payload,
    column_payload,
    packed_mask_words,
    fractured_bit_words,
    own_tile_list,
    active_slot_flags,
):
    unbroken_flags, ref_len, cur_len, stretch, cur_vec = bond_geometry(
        row_payload,
        column_payload,
        packed_mask_words,
        fractured_bit_words,
        own_tile_list,
        active_slot_flags,
    )
    weighted = unbroken_flags * stretch
    return (jnp.sum(weighted, axis=2), jnp.sum(weighted, axis=1))


def force_contributions(
    row_payload,
    column_payload,
    packed_mask_words,
    fractured_bit_words,
    own_tile_list,
    active_slot_flags,
    row_dilatation,
    column_dilatation,
):
    unbroken_flags, ref_len, cur_len, stretch, cur_vec = bond_geometry(
        row_payload,
        column_payload,
        packed_mask_words,
        fractured_bit_words,
        own_tile_list,
        active_slot_flags,
    )
    per_unit_length = shear_term * stretch / ref_len
    gathered_row = (
        unbroken_flags
        * (volumetric_term * row_dilatation[:, :, None] + per_unit_length)
        / row_payload[6][:, :, None]
    )
    gathered_column = (
        unbroken_flags
        * (volumetric_term * column_dilatation[:, None, :] + per_unit_length)
        / column_payload[6][:, None, :]
    )
    weight = (gathered_row + gathered_column) / cur_len
    pair_force = weight[None] * cur_vec
    return (jnp.sum(pair_force, axis=3), -jnp.sum(pair_force, axis=2))


def sweep(kernel, pieces, buffers, total_blocks, block_width):

    def advance(block_index, outputs):
        offset = block_index * block_width
        sliced = [
            lax.dynamic_slice_in_dim(member, offset, block_width, dimension)
            for member, dimension in pieces
        ]
        results = kernel(*sliced)
        return tuple(
            (
                lax.dynamic_update_slice_in_dim(output, result, offset, dimension)
                for output, result, (unused, dimension) in zip(outputs, results, buffers)
            )
        )

    initial = tuple((member for member, dimension in buffers))
    return lax.fori_loop(0, total_blocks, advance, initial)


def send_back(ghost_part):
    channels = ghost_part.shape[0]
    ghost_tile_count = ghost_part.shape[2]
    rotation_index = jnp.array(cycle_cells, dtype=jnp.int32)
    cycle_block = (
        jnp.zeros((channels, 16, ghost_tile_count, 128), jnp.float32)
        .at[:, rotation_index]
        .set(ghost_part)
    )
    cycle_block = cycle_block.reshape(channels, 4, 4, ghost_tile_count, 128)
    corner_sums = []
    widened = extended(cycle_block, (("slab", 1), ("thick", 2)), 1)
    for slab_side in range(2):
        for thick_side in range(2):
            corner_sums.append(
                widened[:, 5 * slab_side, 2 + thick_side]
                + widened[:, 2 + slab_side, 5 * thick_side]
                + widened[:, 5 * slab_side, 5 * thick_side]
            )
    return jnp.stack(corner_sums, 1)


def body(
    ref_pos,
    displacement,
    weighted_volume,
    ghost_corner_lists,
    bond_row_tiles,
    bond_column_tiles,
    bond_count,
    bond_masks,
    broken_bonds,
):
    point_count = ref_pos.shape[1]
    tile_count = point_count // 128
    ghost_tile_count = ghost_corner_lists.shape[2]
    slot_count = bond_row_tiles.shape[0]
    block_width = min(8, slot_count)
    rotation_index = jnp.array(cycle_cells, dtype=jnp.int32)
    point_state = jnp.concatenate([ref_pos, displacement, weighted_volume[None]], 0).reshape(
        7, tile_count, 128
    )
    outgoing = jnp.take(point_state, ghost_corner_lists, axis=1)
    widened = extended(outgoing, (("slab", 1), ("thick", 2)), 1)
    ghosts = widened.reshape(7, 16, ghost_tile_count, 128)[:, rotation_index].reshape(
        7, 12 * ghost_tile_count, 128
    )
    tile_table = jnp.concatenate([point_state, ghosts], 1)
    row_payload = jnp.take(point_state, bond_row_tiles, axis=1)
    column_payload = jnp.take(tile_table, bond_column_tiles, axis=1)
    own_tile_list = bond_column_tiles == bond_row_tiles
    active_slot_flags = jnp.arange(slot_count) < bond_count[0]
    total_blocks = (bond_count[0] + block_width - 1) // block_width
    row_hot = (bond_row_tiles[:, None] == jnp.arange(tile_count)[None, :]).astype(jnp.float32)
    col_hot = (
        bond_column_tiles[:, None] == jnp.arange(tile_count + 12 * ghost_tile_count)[None, :]
    ).astype(jnp.float32)
    box_hot = (
        ghost_corner_lists.reshape(4 * ghost_tile_count)[:, None] == jnp.arange(tile_count)[None, :]
    ).astype(jnp.float32)

    def to_owners(row_term, col_term):
        owned = jnp.einsum("kt,ckp->ctp", row_hot, row_term, precision=highest)
        table_sum = jnp.einsum("kt,ckp->ctp", col_hot, col_term, precision=highest)
        channels = row_term.shape[0]
        returned = send_back(
            table_sum[:, tile_count:].reshape(channels, 12, ghost_tile_count, 128)
        ).reshape(channels, 4 * ghost_tile_count, 128)
        return (
            owned
            + table_sum[:, :tile_count]
            + jnp.einsum("gt,cgp->ctp", box_hot, returned, precision=highest)
        )

    initial_fragments = (
        (row_payload, 1),
        (column_payload, 1),
        (bond_masks, 0),
        (broken_bonds, 0),
        (own_tile_list, 0),
        (active_slot_flags, 0),
    )
    zeros_one = jnp.zeros((slot_count, 128), jnp.float32)
    row_sum, col_sum = sweep(
        stretch_terms,
        initial_fragments,
        ((zeros_one, 0), (zeros_one, 0)),
        total_blocks,
        block_width,
    )
    stretch_sum = to_owners(row_sum[None], col_sum[None])[0]
    dilatation = 3.0 * stretch_sum / point_state[6]
    departing_dilatation = jnp.take(dilatation, ghost_corner_lists, axis=0)
    expanded_dilatation = extended(departing_dilatation, (("slab", 0), ("thick", 1)), 1)
    ghost_dilatations = expanded_dilatation.reshape(16, ghost_tile_count, 128)[
        rotation_index
    ].reshape(12 * ghost_tile_count, 128)
    dilatation_lookup = jnp.concatenate([dilatation, ghost_dilatations], 0)
    row_dilatation = jnp.take(dilatation, bond_row_tiles, axis=0)
    column_dilatation = jnp.take(dilatation_lookup, bond_column_tiles, axis=0)
    zeros_three = jnp.zeros((3, slot_count, 128), jnp.float32)
    row_force, col_force = sweep(
        force_contributions,
        initial_fragments + ((row_dilatation, 0), (column_dilatation, 0)),
        ((zeros_three, 1), (zeros_three, 1)),
        total_blocks,
        block_width,
    )
    force = to_owners(row_force, col_force).reshape(3, point_count)
    return (force, dilatation.reshape(point_count))


def solution(mesh):
    in_specs = (
        P(None, ("slab", "thick")),
        P(None, ("slab", "thick")),
        P(("slab", "thick")),
        P(None, None, ("slab", "thick")),
        P(("slab", "thick")),
        P(("slab", "thick")),
        P(("slab", "thick")),
        P(("slab", "thick"), None, None),
        P(("slab", "thick"), None, None),
    )
    out_specs = (P(None, ("slab", "thick")), P(("slab", "thick")))
    return jax.shard_map(body, mesh=mesh, in_specs=in_specs, out_specs=out_specs, check_vma=False)
```

profile of v0, /device:TPU:5, one launch (start us, length us, event | category | flops | bytes accessed | tf_op | source)
XLA Modules:
  0.0 225.6 jit_solution(18074155172997834948)
XLA Ops:
  4.2 3.1 %collective-permute-start = (f32[7,1,2,16,128]{4,0,3,2,1:T(8,128)S(1)}, f32[7,1,2,16,128]{4,0,3,2,1:T(8,128)S(1)}, u32[]{:S(2)}, u32[]{:S(2)}) collective-permute-start(f32[7,1,2,16,128]{4,0,3,2,1:T(8,128)S(1)} %get-tuple-element.262), channel_id=1, source_target_pairs={{0,4},{4,8},{8,12},{12,16},{16,20},{20,24},{24,28},{1,5},{5,9},{9,... | collective-permute-start | bytes 344072 | tf_op jit(solution)/shard_map/ppermute | solution.py:22
  7.3 2.1 collective-permute-start.1
  10.4 3.5 %collective-permute-done.1 = f32[7,1,2,16,128]{4,0,3,2,1:T(8,128)S(1)} collective-permute-done((f32[7,1,2,16,128]{4,0,3,2,1:T(8,128)S(1)}, f32[7,1,2,16,128]{4,0,3,2,1:T(8,128)S(1)}, u32[]{:S(2)}, u32[]{:S(2)}) %collective-permute-start.1) | collective-permute-done | bytes 114720 | tf_op jit(solution)/shard_map/ppermute | solution.py:25
  14.1 5.1 %collective-permute-start.2 = (f32[7,4,1,16,128]{4,0,3,2,1:T(8,128)S(1)}, f32[7,4,1,16,128]{4,0,3,2,1:T(8,128)S(1)}, u32[]{:S(2)}, u32[]{:S(2)}) collective-permute-start(f32[7,4,1,16,128]{4,0,3,2,1:T(8,128)S(1)} %get-tuple-element.258), channel_id=1, source_target_pairs={{0,1},{1,2},{2,3},{4,5},{5,6},{6,7},{8,9},{9,10},{10,11},{12,13},{... | collective-permute-start | bytes 688136 | tf_op jit(solution)/shard_map/ppermute | solution.py:22
  19.2 1.9 collective-permute-start.3
  22.5 4.4 %collective-permute-done.3 = f32[7,4,1,16,128]{4,0,3,2,1:T(8,128)S(1)} collective-permute-done((f32[7,4,1,16,128]{4,0,3,2,1:T(8,128)S(1)}, f32[7,4,1,16,128]{4,0,3,2,1:T(8,128)S(1)}, u32[]{:S(2)}, u32[]{:S(2)}) %collective-permute-start.3) | collective-permute-done | bytes 229408 | tf_op jit(solution)/shard_map/ppermute | solution.py:25
  30.4 28.9 %while.24 = (s32[]{:T(128)}, f32[128,128]{1,0:T(8,128)S(1)}, f32[128,128]{1,0:T(8,128)S(1)}, s32[]{:T(128)}, pred[128]{0:T(512)(128)(4,1)S(1)}, /*index=5*/pred[...) while((s32[]{:T(128)}, f32[128,128]{1,0:T(8,128)S(1)}, ...), condition=%wide.region_5.6_spmd, body=%wide.region_0.5_spmd.sunk | while | flops 4733191 | bytes 2702099 | solution.py:133
  60.5 25.2 %collective-permute-start.4 = (f32[1,1,4,16,128]{4,3,2,1,0:T(8,128)S(1)}, f32[1,1,4,16,128]{4,3,2,1,0:T(8,128)S(1)}, u32[]{:S(2)}, u32[]{:S(2)}) collective-permute-start(f32[1,1,4,16,128]{4,3,2,1,0:T(8,128)S(1)} %get-tuple-element.272), channel_id=1, source_target_pairs={{0,4},{4,8},{8,12},{12,16},{16,20},{20,24},{24,28},{1,5},{5,9},{9,... | collective-permute-start | bytes 98312 | tf_op jit(solution)/shard_map/ppermute | solution.py:22
  85.8 1.9 collective-permute-start.5
  87.8 3.5 %collective-permute-done.5 = f32[1,1,4,16,128]{4,3,2,1,0:T(8,128)S(1)} collective-permute-done((f32[1,1,4,16,128]{4,3,2,1,0:T(8,128)S(1)}, f32[1,1,4,16,128]{4,3,2,1,0:T(8,128)S(1)}, u32[]{:S(2)}, u32[]{:S(2)}) %collective-permute-start.5) | collective-permute-done | bytes 32800 | tf_op jit(solution)/shard_map/ppermute | solution.py:25
  91.3 2.1 collective-permute-start.6
  93.5 2.2 collective-permute-start.7
  96.0 2.9 %collective-permute-done.7 = f32[1,6,1,16,128]{4,3,2,1,0:T(8,128)S(1)} collective-permute-done((f32[1,6,1,16,128]{4,3,2,1,0:T(8,128)S(1)}, f32[1,6,1,16,128]{4,3,2,1,0:T(8,128)S(1)}, u32[]{:S(2)}, u32[]{:S(2)}) %collective-permute-start.7) | collective-permute-done | bytes 49184 | tf_op jit(solution)/shard_map/ppermute | solution.py:25
  99.9 3.6 %collective-permute-start.8 = (f32[1,2,16,128]{3,2,1,0:T(8,128)S(1)}, f32[1,2,16,128]{3,2,1,0:T(8,128)S(1)}, u32[]{:S(2)}, u32[]{:S(2)}) collective-permute-start(f32[1,2,16,128]{3,2,1,0:T(8,128)S(1)} %get-tuple-element.282), channel_id=1, source_target_pairs={{0,4},{4,8},{8,12},{12,16},{16,20},{20,24},{24,28},{1,5},{5,9},{9,... | collective-permute-start | bytes 49160 | tf_op jit(solution)/shard_map/ppermute | solution.py:22
  103.6 1.9 collective-permute-start.9
  106.2 2.8 %collective-permute-done.9 = f32[1,2,16,128]{3,2,1,0:T(8,128)S(1)} collective-permute-done((f32[1,2,16,128]{3,2,1,0:T(8,128)S(1)}, f32[1,2,16,128]{3,2,1,0:T(8,128)S(1)}, u32[]{:S(2)}, u32[]{:S(2)}) %collective-permute-start.9) | collective-permute-done | bytes 16416 | tf_op jit(solution)/shard_map/ppermute | solution.py:25
  109.0 3.3 %collective-permute-start.10 = (f32[4,1,16,128]{3,2,1,0:T(8,128)S(1)}, f32[4,1,16,128]{3,2,1,0:T(8,128)S(1)}, u32[]{:S(2)}, u32[]{:S(2)}) collective-permute-start(f32[4,1,16,128]{3,2,1,0:T(8,128)S(1)} %get-tuple-element.274), channel_id=1, source_target_pairs={{0,1},{1,2},{2,3},{4,5},{5,6},{6,7},{8,9},{9,10},{10,11},{12,13},{... | collective-permute-start | bytes 98312 | tf_op jit(solution)/shard_map/ppermute | solution.py:22
  112.3 1.9 collective-permute-start.11
  114.3 3.2 %collective-permute-done.11 = f32[4,1,16,128]{3,2,1,0:T(8,128)S(1)} collective-permute-done((f32[4,1,16,128]{3,2,1,0:T(8,128)S(1)}, f32[4,1,16,128]{3,2,1,0:T(8,128)S(1)}, u32[]{:S(2)}, u32[]{:S(2)}) %collective-permute-start.11) | collective-permute-done | bytes 32800 | tf_op jit(solution)/shard_map/ppermute | solution.py:25
  118.9 48.6 %while.25 = (s32[]{:T(128)}, f32[3,128,128]{2,1,0:T(8,128)S(1)}, f32[3,128,128]{2,1,0:T(8,128)S(1)}, s32[]{:T(128)}, pred[128]{0:T(512)(128)(4,1)S(1)}, /*index=...) while((s32[]{:T(128)}, f32[3,128,128]{2,1,0:T(8,128)S(1)}, ...), condition=%wide.region_12.13_spmd, body=%wide.region_7.12_spmd.sunk | while | flops 8010760 | bytes 3893591 | solution.py:133
  169.6 39.5 %collective-permute-start.12 = (f32[3,1,4,16,128]{4,3,0,2,1:T(8,128)S(1)}, f32[3,1,4,16,128]{4,3,0,2,1:T(8,128)S(1)}, u32[]{:S(2)}, u32[]{:S(2)}) collective-permute-start(f32[3,1,4,16,128]{4,3,0,2,1:T(8,128)S(1)} %copy.76), channel_id=1, source_target_pairs={{0,4},{4,8},{8,12},{12,16},{16,20},{20,24},{24,28},{1,5},{5,9},{9,... | collective-permute-start | bytes 294920 | tf_op jit(solution)/shard_map/ppermute | solution.py:22
  211.1 4.3 %collective-permute-done.13 = f32[3,1,4,16,128]{4,3,0,2,1:T(8,128)S(1)} collective-permute-done((f32[3,1,4,16,128]{4,3,0,2,1:T(8,128)S(1)}, f32[3,1,4,16,128]{4,3,0,2,1:T(8,128)S(1)}, u32[]{:S(2)}, u32[]{:S(2)}) %collective-permute-start.13) | collective-permute-done | bytes 98336 | tf_op jit(solution)/shard_map/ppermute | solution.py:25
  217.3 2.4 %collective-permute-start.15 = (f32[3,6,1,16,128]{4,3,0,2,1:T(8,128)S(1)}, f32[3,6,1,16,128]{4,3,0,2,1:T(8,128)S(1)}, u32[]{:S(2)}, u32[]{:S(2)}) collective-permute-start(f32[3,6,1,16,128]{4,3,0,2,1:T(8,128)S(1)} %get-tuple-element.257), channel_id=1, source_target_pairs={{1,0},{2,1},{3,2},{5,4},{6,5},{7,6},{9,8},{10,9},{11,10},{13,12},{... | collective-permute-start | bytes 442376 | tf_op jit(solution)/shard_map/ppermute | solution.py:25
  220.4 3.4 %collective-permute-done.15 = f32[3,6,1,16,128]{4,3,0,2,1:T(8,128)S(1)} collective-permute-done((f32[3,6,1,16,128]{4,3,0,2,1:T(8,128)S(1)}, f32[3,6,1,16,128]{4,3,0,2,1:T(8,128)S(1)}, u32[]{:S(2)}, u32[]{:S(2)}) %collective-permute-start.15) | collective-permute-done | bytes 147488 | tf_op jit(solution)/shard_map/ppermute | solution.py:25
  (387 shorter events, 97.4 us)
Async XLA Ops:
  2.1 7.4 %copy-start.4 = (s32[12]{0:T(128)S(1)}, s32[12]{0:T(128)}, u32[]{:S(2)}) copy-start(s32[12]{0:T(128)} %constant.158) | copy-start | bytes 148
  2.1 7.4 %copy-start.5 = (s32[128]{0:T(128)S(1)}, s32[128]{0:T(128)}, u32[]{:S(2)}) copy-start(s32[128]{0:T(128)} %param.21) | copy-start | bytes 1540
  2.1 7.4 %copy-start.6 = (s32[128]{0:T(128)S(1)}, s32[128]{0:T(128)}, u32[]{:S(2)}) copy-start(s32[128]{0:T(128)} %param.20) | copy-start | bytes 1540
  4.2 6.3 %collective-permute-start = (f32[7,1,2,16,128]{4,0,3,2,1:T(8,128)S(1)}, f32[7,1,2,16,128]{4,0,3,2,1:T(8,128)S(1)}, u32[]{:S(2)}, u32[]{:S(2)}) collective-permute-start(f32[7,1,2,16,128]{4,0,3,2,1:T(8,128)S(1)} %get-tuple-element.262), channel_id=1, source_target_pairs={{0,4},{4,8},{8,12},{12,16},{16,20},{20,24},{24,28},{1,5},{5,9},{9,... | collective-permute-start | bytes 344072 | tf_op jit(solution)/shard_map/ppermute | solution.py:22
  7.3 6.6 %collective-permute-start.1 = (f32[7,1,2,16,128]{4,0,3,2,1:T(8,128)S(1)}, f32[7,1,2,16,128]{4,0,3,2,1:T(8,128)S(1)}, u32[]{:S(2)}, u32[]{:S(2)}) collective-permute-start(f32[7,1,2,16,128]{4,0,3,2,1:T(8,128)S(1)} %get-tuple-element.263), channel_id=1, source_target_pairs={{4,0},{8,4},{12,8},{16,12},{20,16},{24,20},{28,24},{5,1},{9,5},{13... | collective-permute-start | bytes 344072 | tf_op jit(solution)/shard_map/ppermute | solution.py:25
  14.1 8.4 %collective-permute-start.2 = (f32[7,4,1,16,128]{4,0,3,2,1:T(8,128)S(1)}, f32[7,4,1,16,128]{4,0,3,2,1:T(8,128)S(1)}, u32[]{:S(2)}, u32[]{:S(2)}) collective-permute-start(f32[7,4,1,16,128]{4,0,3,2,1:T(8,128)S(1)} %get-tuple-element.258), channel_id=1, source_target_pairs={{0,1},{1,2},{2,3},{4,5},{5,6},{6,7},{8,9},{9,10},{10,11},{12,13},{... | collective-permute-start | bytes 688136 | tf_op jit(solution)/shard_map/ppermute | solution.py:22
  19.2 7.7 %collective-permute-start.3 = (f32[7,4,1,16,128]{4,0,3,2,1:T(8,128)S(1)}, f32[7,4,1,16,128]{4,0,3,2,1:T(8,128)S(1)}, u32[]{:S(2)}, u32[]{:S(2)}) collective-permute-start(f32[7,4,1,16,128]{4,0,3,2,1:T(8,128)S(1)} %get-tuple-element.259), channel_id=1, source_target_pairs={{1,0},{2,1},{3,2},{5,4},{6,5},{7,6},{9,8},{10,9},{11,10},{13,12},{... | collective-permute-start | bytes 688136 | tf_op jit(solution)/shard_map/ppermute | solution.py:25
  27.8 1.0 copy-start
  27.8 1.0 copy-start.1
  27.8 1.0 copy-start.2
  30.4 57.3 %copy-start.3 = (s32[2,2,16]{2,1,0:T(2,128)S(1)}, s32[2,2,16]{2,1,0:T(2,128)}, u32[]{:S(2)}) copy-start(s32[2,2,16]{2,1,0:T(2,128)} %param.19) | copy-start | bytes 772
  60.5 27.3 %collective-permute-start.4 = (f32[1,1,4,16,128]{4,3,2,1,0:T(8,128)S(1)}, f32[1,1,4,16,128]{4,3,2,1,0:T(8,128)S(1)}, u32[]{:S(2)}, u32[]{:S(2)}) collective-permute-start(f32[1,1,4,16,128]{4,3,2,1,0:T(8,128)S(1)} %get-tuple-element.272), channel_id=1, source_target_pairs={{0,4},{4,8},{8,12},{12,16},{16,20},{20,24},{24,28},{1,5},{5,9},{9,... | collective-permute-start | bytes 98312 | tf_op jit(solution)/shard_map/ppermute | solution.py:22
  85.8 5.6 %collective-permute-start.5 = (f32[1,1,4,16,128]{4,3,2,1,0:T(8,128)S(1)}, f32[1,1,4,16,128]{4,3,2,1,0:T(8,128)S(1)}, u32[]{:S(2)}, u32[]{:S(2)}) collective-permute-start(f32[1,1,4,16,128]{4,3,2,1,0:T(8,128)S(1)} %get-tuple-element.273), channel_id=1, source_target_pairs={{4,0},{8,4},{12,8},{16,12},{20,16},{24,20},{28,24},{5,1},{9,5},{13... | collective-permute-start | bytes 98312 | tf_op jit(solution)/shard_map/ppermute | solution.py:25
  91.3 4.7 %collective-permute-start.6 = (f32[1,6,1,16,128]{4,3,2,1,0:T(8,128)S(1)}, f32[1,6,1,16,128]{4,3,2,1,0:T(8,128)S(1)}, u32[]{:S(2)}, u32[]{:S(2)}) collective-permute-start(f32[1,6,1,16,128]{4,3,2,1,0:T(8,128)S(1)} %get-tuple-element.264), channel_id=1, source_target_pairs={{0,1},{1,2},{2,3},{4,5},{5,6},{6,7},{8,9},{9,10},{10,11},{12,13},{... | collective-permute-start | bytes 147464 | tf_op jit(solution)/shard_map/ppermute | solution.py:22
  93.5 5.4 %collective-permute-start.7 = (f32[1,6,1,16,128]{4,3,2,1,0:T(8,128)S(1)}, f32[1,6,1,16,128]{4,3,2,1,0:T(8,128)S(1)}, u32[]{:S(2)}, u32[]{:S(2)}) collective-permute-start(f32[1,6,1,16,128]{4,3,2,1,0:T(8,128)S(1)} %get-tuple-element.265), channel_id=1, source_target_pairs={{1,0},{2,1},{3,2},{5,4},{6,5},{7,6},{9,8},{10,9},{11,10},{13,12},{... | collective-permute-start | bytes 147464 | tf_op jit(solution)/shard_map/ppermute | solution.py:25
  99.9 6.2 %collective-permute-start.8 = (f32[1,2,16,128]{3,2,1,0:T(8,128)S(1)}, f32[1,2,16,128]{3,2,1,0:T(8,128)S(1)}, u32[]{:S(2)}, u32[]{:S(2)}) collective-permute-start(f32[1,2,16,128]{3,2,1,0:T(8,128)S(1)} %get-tuple-element.282), channel_id=1, source_target_pairs={{0,4},{4,8},{8,12},{12,16},{16,20},{20,24},{24,28},{1,5},{5,9},{9,... | collective-permute-start | bytes 49160 | tf_op jit(solution)/shard_map/ppermute | solution.py:22
  103.6 5.4 %collective-permute-start.9 = (f32[1,2,16,128]{3,2,1,0:T(8,128)S(1)}, f32[1,2,16,128]{3,2,1,0:T(8,128)S(1)}, u32[]{:S(2)}, u32[]{:S(2)}) collective-permute-start(f32[1,2,16,128]{3,2,1,0:T(8,128)S(1)} %get-tuple-element.283), channel_id=1, source_target_pairs={{4,0},{8,4},{12,8},{16,12},{20,16},{24,20},{28,24},{5,1},{9,5},{13... | collective-permute-start | bytes 49160 | tf_op jit(solution)/shard_map/ppermute | solution.py:25
  109.0 5.3 %collective-permute-start.10 = (f32[4,1,16,128]{3,2,1,0:T(8,128)S(1)}, f32[4,1,16,128]{3,2,1,0:T(8,128)S(1)}, u32[]{:S(2)}, u32[]{:S(2)}) collective-permute-start(f32[4,1,16,128]{3,2,1,0:T(8,128)S(1)} %get-tuple-element.274), channel_id=1, source_target_pairs={{0,1},{1,2},{2,3},{4,5},{5,6},{6,7},{8,9},{9,10},{10,11},{12,13},{... | collective-permute-start | bytes 98312 | tf_op jit(solution)/shard_map/ppermute | solution.py:22
  112.3 5.2 %collective-permute-start.11 = (f32[4,1,16,128]{3,2,1,0:T(8,128)S(1)}, f32[4,1,16,128]{3,2,1,0:T(8,128)S(1)}, u32[]{:S(2)}, u32[]{:S(2)}) collective-permute-start(f32[4,1,16,128]{3,2,1,0:T(8,128)S(1)} %get-tuple-element.275), channel_id=1, source_target_pairs={{1,0},{2,1},{3,2},{5,4},{6,5},{7,6},{9,8},{10,9},{11,10},{13,12},{... | collective-permute-start | bytes 98312 | tf_op jit(solution)/shard_map/ppermute | solution.py:25
  169.6 41.4 %collective-permute-start.12 = (f32[3,1,4,16,128]{4,3,0,2,1:T(8,128)S(1)}, f32[3,1,4,16,128]{4,3,0,2,1:T(8,128)S(1)}, u32[]{:S(2)}, u32[]{:S(2)}) collective-permute-start(f32[3,1,4,16,128]{4,3,0,2,1:T(8,128)S(1)} %copy.76), channel_id=1, source_target_pairs={{0,4},{4,8},{8,12},{12,16},{16,20},{20,24},{24,28},{1,5},{5,9},{9,... | collective-permute-start | bytes 294920 | tf_op jit(solution)/shard_map/ppermute | solution.py:22
  209.1 6.3 %collective-permute-start.13 = (f32[3,1,4,16,128]{4,3,0,2,1:T(8,128)S(1)}, f32[3,1,4,16,128]{4,3,0,2,1:T(8,128)S(1)}, u32[]{:S(2)}, u32[]{:S(2)}) collective-permute-start(f32[3,1,4,16,128]{4,3,0,2,1:T(8,128)S(1)} %copy.77), channel_id=1, source_target_pairs={{4,0},{8,4},{12,8},{16,12},{20,16},{24,20},{28,24},{5,1},{9,5},{13... | collective-permute-start | bytes 294920 | tf_op jit(solution)/shard_map/ppermute | solution.py:25
  215.4 5.0 %collective-permute-start.14 = (f32[3,6,1,16,128]{4,3,0,2,1:T(8,128)S(1)}, f32[3,6,1,16,128]{4,3,0,2,1:T(8,128)S(1)}, u32[]{:S(2)}, u32[]{:S(2)}) collective-permute-start(f32[3,6,1,16,128]{4,3,0,2,1:T(8,128)S(1)} %get-tuple-element.256), channel_id=1, source_target_pairs={{0,1},{1,2},{2,3},{4,5},{5,6},{6,7},{8,9},{9,10},{10,11},{12,13},{... | collective-permute-start | bytes 442376 | tf_op jit(solution)/shard_map/ppermute | solution.py:22
  217.3 6.5 %collective-permute-start.15 = (f32[3,6,1,16,128]{4,3,0,2,1:T(8,128)S(1)}, f32[3,6,1,16,128]{4,3,0,2,1:T(8,128)S(1)}, u32[]{:S(2)}, u32[]{:S(2)}) collective-permute-start(f32[3,6,1,16,128]{4,3,0,2,1:T(8,128)S(1)} %get-tuple-element.257), channel_id=1, source_target_pairs={{1,0},{2,1},{3,2},{5,4},{6,5},{7,6},{9,8},{10,9},{11,10},{13,12},{... | collective-permute-start | bytes 442376 | tf_op jit(solution)/shard_map/ppermute | solution.py:25
where the time goes:
time: 228 us; the launch traced here: 226 us
  starting transfers between devices  100 us (44%)
  other arithmetic  50.5 us (22%)
  local copies, waits for them, and re-layouts  40.2 us (18%)
  waiting for transfers between devices  28.7 us (13%)
    ppermute x8, starting transfers between devices, extended(): lax.ppermute(lax.slice_in_dim(block, block.shape[dim] - width, None, axis...  84 us
    ppermute x8, waiting for transfers between devices, extended(): lax.ppermute(lax.slice_in_dim(block, 0, width, axis=dim), axis, backward)  28 us
    dynamic_slice x63, local copies, waits for them, and re-layouts, advance(): lax.dynamic_slice_in_dim(member, offset, block_width, dimension)  26.1 us
    reduce_sum x18, other arithmetic, bond_geometry(): jnp.sum(cur_vec * cur_vec, axis=0)  18.8 us
    ppermute x8, starting transfers between devices, extended(): lax.ppermute(lax.slice_in_dim(block, 0, width, axis=dim), axis, backward)  16.3 us
    reduce_sum x9, other arithmetic, force_contributions(): return (jnp.sum(pair_force, axis=3), -jnp.sum(pair_force, axis=2))  13.2 us
    div x9, other arithmetic, force_contributions(): weight = (gathered_row + gathered_column) / cur_len  6.97 us
    reduce_sum x9, other arithmetic, stretch_terms(): return (jnp.sum(weighted, axis=2), jnp.sum(weighted, axis=1))  5.76 us
  transfers between devices with their start and end apart: 16, of which 10 were waited for; matrix products, arithmetic and copies ran while one was open for 1% of the time, Pallas kernels for 0%

commit v1 on v0

v1 whole, which is shorter than its diff:
```python
import functools

import jax
import jax.numpy as jnp
from jax import lax
from jax.experimental import pallas as pl
from jax.experimental.pallas import tpu as pltpu
from jax.sharding import PartitionSpec as P

young = 25.0
poisson = 0.22
bulk_modulus = young / (3.0 * (1.0 - 2.0 * poisson))
shear_modulus = young / (2.0 * (1.0 + poisson))
volumetric_term = 3.0 * bulk_modulus - 5.0 * shear_modulus
shear_term = 15.0 * shear_modulus
floor_squared = 0.25
centre = 4.0
cycle_cells = (0, 1, 2, 3, 4, 7, 8, 11, 12, 13, 14, 15)
MESH = pl.DeviceIdType.MESH
f32, bf16 = jnp.float32, jnp.bfloat16
UNROLL = 2
NN = (((1,), (0,)), ((), ()))
NT = (((1,), (1,)), ((), ()))
TN = (((0,), (0,)), ((), ()))


def cell_plan():
    plan = []
    for cell in cycle_cells:
        row, col = cell // 4, cell % 4
        step = (-1, 0, 0, 1)
        side = (1, 0, 1, 0)
        plan.append((step[row], step[col], 2 * side[row] + side[col]))
    return plan


def dot(a, b, dims):
    return lax.dot_general(a, b, dims, preferred_element_type=f32)


def rounded(x):
    return x.astype(bf16).astype(f32)


def split3(x):
    high = rounded(x)
    rest = x - high
    middle = rounded(rest)
    return high, middle, rest - middle


def split2(x):
    high = x.astype(bf16)
    return high, (x - high.astype(f32)).astype(bf16)


def hot_dot(hot, x):
    high, middle, low = split3(x)
    return (
        dot(hot, high.astype(bf16), NN)
        + dot(hot, middle.astype(bf16), NN)
        + dot(hot, low.astype(bf16), NN)
    )


def features(payload):
    row = lax.broadcasted_iota(jnp.int32, payload.shape, 0)
    high, middle, low = split3(payload)
    square = payload * payload
    cur = jnp.sum(square[0:3], axis=0, keepdims=True)
    ref = jnp.sum(square[4:7], axis=0, keepdims=True)
    norm = jnp.where(row < 4, cur, ref)
    n_high, n_middle, n_low = split3(norm)
    which = row & 3
    norms = jnp.where(
        which == 0, n_high, jnp.where(which == 1, n_middle, jnp.where(which == 2, n_low, 0.0))
    )
    return high, middle, low, norms


def weighted_rows(payload, scale):
    row = lax.broadcasted_iota(jnp.int32, payload.shape, 0)
    both = jnp.where(row < 4, payload, scale * pltpu.roll(payload, 4, 0))
    pieces = jnp.concatenate(split3(both), axis=0).astype(bf16)
    return jnp.concatenate([pieces, pieces], axis=1)


def fold(stacked, scale):
    total = stacked[0:8] + stacked[8:16] + stacked[16:24]
    return scale * total + pltpu.roll(total, 4, 0)


def kernel(
    axes,
    row_ref,
    col_ref,
    count_ref,
    list_ref,
    row_vec,
    col_vec,
    list_vec,
    pos_ref,
    disp_ref,
    vol_ref,
    mask_ref,
    broken_ref,
    force_ref,
    dil_ref,
    tab,
    out_buf,
    ghost_in,
    row_sum,
    col_sum,
    sum_out,
    sum_in,
    alpha_tab,
    alpha_out,
    alpha_in,
    p_high,
    p_low,
    q_row,
    q_col,
    row_force,
    col_force,
    force_out,
    force_in,
    send_sem,
    recv_sem,
):
    slab, thick = axes
    si, ti = lax.axis_index(slab), lax.axis_index(thick)
    n_slab, n_thick = lax.axis_size(slab), lax.axis_size(thick)
    tiles = vol_ref.shape[0]
    slots = row_vec.shape[1]
    g = list_vec.shape[1] // 4
    plan = cell_plan()

    def there(ds, dt):
        s, t = si + ds, ti + dt
        return (s >= 0) & (s < n_slab) & (t >= 0) & (t < n_thick)

    steps = [(a, b) for a in (-1, 0, 1) for b in (-1, 0, 1) if (a, b) != (0, 0)]
    barrier = pltpu.get_barrier_semaphore()
    for ds, dt in steps:

        @pl.when(there(ds, dt))
        def _(ds=ds, dt=dt):
            pl.semaphore_signal(barrier, inc=1, device_id=(si + ds, ti + dt), device_id_type=MESH)

    def copy_of(phase, q, source, target, ds, dt):
        return pltpu.make_async_remote_copy(
            src_ref=source(q),
            dst_ref=target(q),
            send_sem=send_sem.at[phase, q],
            recv_sem=recv_sem.at[phase, q],
            device_id=(si + ds, ti + dt),
            device_id_type=MESH,
        )

    def exchange(phase, source, target, sign):
        for q, (ds, dt, _c) in enumerate(plan):

            @pl.when(there(sign * ds, sign * dt))
            def _(q=q, ds=sign * ds, dt=sign * dt):
                copy_of(phase, q, source, target, ds, dt).start()

    def finish(phase, source, target, sign):
        for q, (ds, dt, _c) in enumerate(plan):

            @pl.when(there(-sign * ds, -sign * dt))
            def _(q=q, ds=-sign * ds, dt=-sign * dt):
                copy_of(phase, q, source, target, ds, dt).wait_recv()

            @pl.when(there(sign * ds, sign * dt))
            def _(q=q, ds=sign * ds, dt=sign * dt):
                copy_of(phase, q, source, target, ds, dt).wait_send()

    for q, (ds, dt, _c) in enumerate(plan):

        @pl.when(jnp.logical_not(there(ds, dt)))
        def _(q=q):
            ghost_in[q * g : (q + 1) * g] = jnp.zeros((g, 8, 128), f32)
            alpha_in[q * g : (q + 1) * g] = jnp.zeros((g, 128), f32)

        @pl.when(jnp.logical_not(there(-ds, -dt)))
        def _(q=q):
            sum_in[q] = jnp.zeros((g, 128), f32)
            force_in[q] = jnp.zeros((g, 384), f32)

    def build(t, carry):
        at = pl.ds(pl.multiple_of(t * 128, 128), 128)
        ref = pos_ref[:, at] - centre
        tab[t] = jnp.concatenate(
            [
                ref + disp_ref[:, at],
                jnp.ones((1, 128), f32),
                ref,
                shear_term / vol_ref[pl.ds(t, 1), :],
            ],
            axis=0,
        )
        return carry

    lax.fori_loop(0, tiles, build, 0, unroll=4)

    for s in range(2):
        for t in range(2):

            def pick(i, carry, s=s, t=t):
                out_buf[(2 * s + t) * g + i] = tab[list_ref[s, t, i]]
                return carry

            lax.fori_loop(0, g, pick, 0, unroll=4)

    peers = sum(there(ds, dt).astype(jnp.int32) for ds, dt in steps)
    pl.semaphore_wait(barrier, peers)

    corner = [c for _s, _t, c in plan]
    payload = (
        0,
        lambda q: out_buf.at[corner[q] * g : (corner[q] + 1) * g],
        lambda q: ghost_in.at[q * g : (q + 1) * g],
        -1,
    )
    exchange(*payload)
    finish(*payload)
    tab[tiles:] = ghost_in[...]

    sub = lax.broadcasted_iota(jnp.int32, (8, 128), 0)
    cur_rows = (sub < 3).astype(f32)
    ref_rows = ((sub >= 4) & (sub < 7)).astype(f32)
    one8 = jnp.ones((8, 128), f32)
    ones = jnp.ones((8, 256), bf16)
    word = lax.broadcasted_iota(jnp.int32, (16, 128), 0)
    lane = lax.broadcasted_iota(jnp.int32, (16, 128), 1)
    triangle = (1 << jnp.clip(lane - 8 * word, 0, 8)) - 1
    bit = lax.broadcasted_iota(jnp.int32, (16, 8, 128), 1)
    live = count_ref[0]

    def first(k):
        a, b = row_ref[k], col_ref[k]
        vi, vj = tab[a], tab[b]
        hi, mi, li, ni = features(vi)
        hj, mj, lj, nj = features(vj)
        left = jnp.concatenate([hi, hi, mi, mi, hi, li, ni, one8], axis=0).astype(bf16)
        hj, mj, lj = -2.0 * hj, -2.0 * mj, -2.0 * lj
        base = (hj, mj, hj, mj, lj, hj, one8, nj)
        right = jnp.concatenate(
            [
                jnp.concatenate([x * ref_rows for x in base], axis=0),
                jnp.concatenate([x * cur_rows for x in base], axis=0),
            ],
            axis=1,
        ).astype(bf16)
        squares = jnp.maximum(dot(left, right, TN), floor_squared)
        ref_sq, cur_sq = squares[:, 0:128], squares[:, 128:256]
        ref_inv, cur_inv = lax.rsqrt(ref_sq), lax.rsqrt(cur_sq)
        words = mask_ref[k] & ~broken_ref[k]
        words = words & jnp.where(a == b, triangle, 255)
        words = words & jnp.where(k < live, 255, 0)
        spread = jnp.broadcast_to(words[:, None, :], (16, 8, 128))
        keep = ((spread & (1 << bit)) != 0).reshape(128, 128)
        e = jnp.where(keep, cur_sq * cur_inv - ref_sq * ref_inv, 0.0)
        p = jnp.where(keep, cur_inv, 0.0)
        q = jnp.where(keep, ref_inv - cur_inv, 0.0)
        col_sum[pl.ds(k, 1), :] = jnp.sum(e, axis=0, keepdims=True)
        row_sum[pl.ds(k, 1), :] = dot(ones, jnp.concatenate(split2(e), axis=1), NT)[0:1]
        ph, plow = split2(p)
        p_high[k] = ph
        p_low[k] = plow
        qh, qlow = split2(q)
        gi, gj = vi[7:8], vj[7:8]
        q_row[k] = fold(
            dot(weighted_rows(vj, gj), jnp.concatenate([qh, qlow], axis=1), NT), gi
        )
        q_col[k] = fold(
            dot(weighted_rows(vi, gi), jnp.concatenate([qh, qlow], axis=0), NN), gj
        )

    def first_loop(block, carry):
        for u in range(UNROLL):
            first(block * UNROLL + u)
        return carry

    lax.fori_loop(0, slots // UNROLL, first_loop, 0)

    row_hot = (
        lax.broadcasted_iota(jnp.int32, (tiles, slots), 0) == row_vec[...]
    ).astype(f32).astype(bf16)
    col_hot = (
        lax.broadcasted_iota(jnp.int32, (tiles + 12 * g, slots), 0) == col_vec[...]
    ).astype(f32).astype(bf16)
    box_hot = (
        lax.broadcasted_iota(jnp.int32, (tiles, 4 * g), 0) == list_vec[...]
    ).astype(f32).astype(bf16)

    def returned(buffer):
        corners = []
        for c in range(4):
            parts = [buffer[q] for q in range(12) if corner[q] == c]
            corners.append(parts[0] + parts[1] + parts[2])
        return hot_dot(box_hot, jnp.concatenate(corners, axis=0))

    col_part = hot_dot(col_hot, col_sum[...])
    sum_out[...] = col_part[tiles:]
    sums = (1, lambda q: sum_out.at[q * g : (q + 1) * g], lambda q: sum_in.at[q], 1)
    exchange(*sums)
    own = hot_dot(row_hot, row_sum[...]) + col_part[:tiles]
    finish(*sums)
    volume = vol_ref[...]
    dilatation = 3.0 * (own + returned(sum_in)) / volume
    dil_ref[...] = dilatation
    alpha_tab[0:tiles] = volumetric_term * dilatation / volume

    for s in range(2):
        for t in range(2):

            def pick_alpha(i, carry, s=s, t=t):
                alpha_out[pl.ds((2 * s + t) * g + i, 1), :] = alpha_tab[
                    pl.ds(list_ref[s, t, i], 1), :
                ]
                return carry

            lax.fori_loop(0, g, pick_alpha, 0, unroll=4)

    alphas = (
        2,
        lambda q: alpha_out.at[corner[q] * g : (corner[q] + 1) * g],
        lambda q: alpha_in.at[q * g : (q + 1) * g],
        -1,
    )
    exchange(*alphas)
    finish(*alphas)
    alpha_tab[tiles:] = alpha_in[...]

    def second(k):
        a, b = row_ref[k], col_ref[k]
        vi, vj = tab[a], tab[b]
        ai, aj = alpha_tab[pl.ds(a, 1), :], alpha_tab[pl.ds(b, 1), :]
        ph, plow = p_high[k], p_low[k]
        rows = q_row[k] + fold(
            dot(weighted_rows(vj, aj), jnp.concatenate([ph, plow], axis=1), NT), ai
        )
        cols = q_col[k] + fold(
            dot(weighted_rows(vi, ai), jnp.concatenate([ph, plow], axis=0), NN), aj
        )
        rows = rows - vi * rows[3:4]
        cols = cols - vj * cols[3:4]
        for c in range(3):
            row_force[c, pl.ds(k, 1), :] = rows[c : c + 1]
            col_force[c, pl.ds(k, 1), :] = cols[c : c + 1]

    def second_loop(block, carry):
        for u in range(UNROLL):
            second(block * UNROLL + u)
        return carry

    lax.fori_loop(0, slots // UNROLL, second_loop, 0)

    col_part = hot_dot(col_hot, jnp.concatenate([col_force[c] for c in range(3)], axis=1))
    force_out[...] = col_part[tiles:]
    forces = (3, lambda q: force_out.at[q * g : (q + 1) * g], lambda q: force_in.at[q], 1)
    exchange(*forces)
    own = hot_dot(row_hot, jnp.concatenate([row_force[c] for c in range(3)], axis=1)) + col_part[:tiles]
    finish(*forces)
    total = own + returned(force_in)
    for c in range(3):
        force_ref[c] = total[:, c * 128 : (c + 1) * 128]


def body(
    ref_pos,
    displacement,
    weighted_volume,
    ghost_corner_lists,
    bond_row_tiles,
    bond_column_tiles,
    bond_count,
    bond_masks,
    broken_bonds,
):
    points = ref_pos.shape[1]
    tiles = points // 128
    g = ghost_corner_lists.shape[2]
    slots = bond_row_tiles.shape[0]
    smem = pl.BlockSpec(memory_space=pltpu.SMEM)
    vmem = pl.BlockSpec(memory_space=pltpu.VMEM)
    force, dilatation = pl.pallas_call(
        functools.partial(kernel, ("slab", "thick")),
        out_shape=(
            jax.ShapeDtypeStruct((3, tiles, 128), f32),
            jax.ShapeDtypeStruct((tiles, 128), f32),
        ),
        in_specs=[smem] * 4 + [vmem] * 8,
        out_specs=(vmem, vmem),
        scratch_shapes=[
            pltpu.VMEM((tiles + 12 * g, 8, 128), f32),
            pltpu.VMEM((4 * g, 8, 128), f32),
            pltpu.VMEM((12 * g, 8, 128), f32),
            pltpu.VMEM((slots, 128), f32),
            pltpu.VMEM((slots, 128), f32),
            pltpu.VMEM((12 * g, 128), f32),
            pltpu.VMEM((12, g, 128), f32),
            pltpu.VMEM((tiles + 12 * g, 128), f32),
            pltpu.VMEM((4 * g, 128), f32),
            pltpu.VMEM((12 * g, 128), f32),
            pltpu.VMEM((slots, 128, 128), bf16),
            pltpu.VMEM((slots, 128, 128), bf16),
            pltpu.VMEM((slots, 8, 128), f32),
            pltpu.VMEM((slots, 8, 128), f32),
            pltpu.VMEM((3, slots, 128), f32),
            pltpu.VMEM((3, slots, 128), f32),
            pltpu.VMEM((12 * g, 384), f32),
            pltpu.VMEM((12, g, 384), f32),
            pltpu.SemaphoreType.DMA((4, 12)),
            pltpu.SemaphoreType.DMA((4, 12)),
        ],
        compiler_params=pltpu.CompilerParams(
            collective_id=0, has_side_effects=True, vmem_limit_bytes=40 * 1024 * 1024
        ),
    )(
        bond_row_tiles,
        bond_column_tiles,
        bond_count,
        ghost_corner_lists,
        bond_row_tiles.reshape(1, slots),
        bond_column_tiles.reshape(1, slots),
        ghost_corner_lists.reshape(1, 4 * g),
        ref_pos,
        displacement,
        weighted_volume.reshape(tiles, 128),
        bond_masks,
        broken_bonds,
    )
    return force.reshape(3, points), dilatation.reshape(points)


def solution(mesh):
    in_specs = (
        P(None, ("slab", "thick")),
        P(None, ("slab", "thick")),
        P(("slab", "thick")),
        P(None, None, ("slab", "thick")),
        P(("slab", "thick")),
        P(("slab", "thick")),
        P(("slab", "thick")),
        P(("slab", "thick"), None, None),
        P(("slab", "thick"), None, None),
    )
    out_specs = (P(None, ("slab", "thick")), P(("slab", "thick")))
    return jax.shard_map(body, mesh=mesh, in_specs=in_specs, out_specs=out_specs, check_vma=False)
```

time: 228 us -> 88.1 us (0.39)
  starting transfers between devices: 100 us -> 0 us
  Pallas kernels: 0 us -> 77.9 us
  other arithmetic: 50.5 us -> 0 us
  local copies, waits for them, and re-layouts: 40.2 us -> 8 us
  waiting for transfers between devices: 28.7 us -> 0 us
    ppermute x16 -> x0, starting transfers between devices: 100 us -> none  [the longest x8 84 us: extended(): lax.ppermute(lax.slice_in_dim(block, block.shape[dim] - width, None, axis...]
    pallas_call x0 -> x1, Pallas kernels: none -> 77.9 us  [body(): pl.pallas_call(functools.partial(kernel, ('slab', 'thick')), out_shape=(j...]
    reduce_sum x36 -> x0, other arithmetic: 37.8 us -> none  [the longest x18 18.8 us: bond_geometry(): jnp.sum(cur_vec * cur_vec, axis=0)]
    ppermute x16 -> x0, waiting for transfers between devices: 28.7 us -> none  [the longest x8 28 us: extended(): lax.ppermute(lax.slice_in_dim(block, 0, width, axis=dim), axis, backward)]
    dynamic_slice x63 -> x0, local copies, waits for them, and re-layouts: 26.1 us -> none  [advance(): lax.dynamic_slice_in_dim(member, offset, block_width, dimension)]
    div x10 -> x0, other arithmetic: 7.62 us -> none  [the longest x9 6.97 us: force_contributions(): weight = (gathered_row + gathered_column) / cur_len]
    unnamed x19 -> x18, local copies, waits for them, and re-layouts: 1.46 us -> 7.92 us
    gather x9 -> x0, local copies, waits for them, and re-layouts: 5.24 us -> none  [the longest x1 0.76 us: body(): row_payload = jnp.take(point_state, bond_row_tiles, axis=1)]
  transfers between devices with their start and end apart: 16 -> 0, of which waited for: 10 -> 0; matrix products, arithmetic and copies ran while one was open for 1% -> 0% of each run, Pallas kernels for 0% -> 0%
where the time goes in v1:
time: 88.1 us; the launch traced here: 87.2 us
  Pallas kernels  77.9 us (88%)
  local copies, waits for them, and re-layouts  8 us (9%)
  between operations  1.3 us (1%)
    pallas_call x1, Pallas kernels, body(): pl.pallas_call(functools.partial(kernel, ('slab', 'thick')), out_shape=(j...  77.9 us
    unnamed x18, local copies, waits for them, and re-layouts  7.92 us

profile of v1, /device:TPU:5, one launch (start us, length us, event | category | flops | bytes accessed | tf_op | source)
XLA Modules:
  0.0 87.2 jit_solution(1348717766609830995)
XLA Ops:
  1.3 0.0 copy-start.5
  1.3 0.7 copy-done.5
  2.0 0.0 copy-start.6
  2.0 0.0 copy-start.7
  2.0 0.1 reshape.24.list_vec
  2.0 0.6 copy-done.6
  2.6 0.0 copy-done.7
  2.6 0.0 copy-start
  2.6 1.2 %copy-done = s32[128,16,128]{2,1,0:T(8,128)S(1)} copy-done((s32[128,16,128]{2,1,0:T(8,128)S(1)}, s32[128,16,128]{2,1,0:T(8,128)}, u32[]{:S(2)}) %copy-start) | copy-done | bytes 1048600
  3.9 0.0 copy-start.1
  3.9 1.2 %copy-done.1 = s32[128,16,128]{2,1,0:T(8,128)S(1)} copy-done((s32[128,16,128]{2,1,0:T(8,128)S(1)}, s32[128,16,128]{2,1,0:T(8,128)}, u32[]{:S(2)}) %copy-start.1) | copy-done | bytes 1048600
  5.1 0.0 copy-start.2
  5.1 0.9 %copy-done.2 = f32[3,16384]{1,0:T(4,128)S(1)} copy-done((f32[3,16384]{1,0:T(4,128)S(1)}, f32[3,16384]{1,0:T(4,128)}, u32[]{:S(2)}) %copy-start.2) | copy-done | bytes 196632
  6.0 0.0 copy-start.3
  6.0 0.9 %copy-done.3 = f32[3,16384]{1,0:T(4,128)S(1)} copy-done((f32[3,16384]{1,0:T(4,128)S(1)}, f32[3,16384]{1,0:T(4,128)}, u32[]{:S(2)}) %copy-start.3) | copy-done | bytes 196632
  7.0 0.0 copy-start.4
  7.0 0.8 copy-done.4
  7.8 77.9 %shard_map.104 = (f32[3,128,128]{2,1,0:T(8,128)S(1)}, f32[128,128]{1,0:T(8,128)S(1)}) custom-call(s32[128]{0:T(128)S(1)} %copy-done.6, s32[128]{0:T(128)S(1)} %copy-done.7, s32[1]{0:T(128)S(6)} %copy.15.count_ref, s32[2,2,16]{2,1,0:T(2,128)S(1)} %copy-done.5, s32[1,128]{1,0:T(1,128)S(1)} %bitcast.11, s32[1,128]{1,0:T(1,128)S(1)} %bitcast.12, ...), custom_call_target="tpu_custom_call" | custom-call | tf_op jit(solution)/shard_map/pallas_call | solution.py:388
  85.8 0.8 copy.13
  86.6 0.6 copy.16
Async XLA Ops:
  1.3 0.7 copy-start.5
  2.0 0.7 copy-start.6
  2.0 0.7 copy-start.7
  2.6 1.2 %copy-start = (s32[128,16,128]{2,1,0:T(8,128)S(1)}, s32[128,16,128]{2,1,0:T(8,128)}, u32[]{:S(2)}) copy-start(s32[128,16,128]{2,1,0:T(8,128)} %mask_ref.1) | copy-start | bytes 3145732
  3.9 1.2 %copy-start.1 = (s32[128,16,128]{2,1,0:T(8,128)S(1)}, s32[128,16,128]{2,1,0:T(8,128)}, u32[]{:S(2)}) copy-start(s32[128,16,128]{2,1,0:T(8,128)} %broken_ref.1) | copy-start | bytes 3145732
  5.1 0.9 %copy-start.2 = (f32[3,16384]{1,0:T(4,128)S(1)}, f32[3,16384]{1,0:T(4,128)}, u32[]{:S(2)}) copy-start(f32[3,16384]{1,0:T(4,128)} %pos_ref.1) | copy-start | bytes 589828
  6.0 0.9 %copy-start.3 = (f32[3,16384]{1,0:T(4,128)S(1)}, f32[3,16384]{1,0:T(4,128)}, u32[]{:S(2)}) copy-start(f32[3,16384]{1,0:T(4,128)} %disp_ref.1) | copy-start | bytes 589828
  7.0 0.8 copy-start.4

commit v2 on v1

--- a/solution.py
+++ b/solution.py
@@ -18,7 +18,7 @@
 cycle_cells = (0, 1, 2, 3, 4, 7, 8, 11, 12, 13, 14, 15)
 MESH = pl.DeviceIdType.MESH
 f32, bf16 = jnp.float32, jnp.bfloat16
-UNROLL = 2
+UNROLL = 4
 NN = (((1,), (0,)), ((), ()))
 NT = (((1,), (1,)), ((), ()))
 TN = (((0,), (0,)), ((), ()))
@@ -102,10 +102,12 @@
     pos_ref,
     disp_ref,
     vol_ref,
+    mask_hbm,
+    broken_hbm,
+    force_ref,
+    dil_ref,
     mask_ref,
     broken_ref,
-    force_ref,
-    dil_ref,
     tab,
     out_buf,
     ghost_in,
@@ -126,7 +128,12 @@
     force_in,
     send_sem,
     recv_sem,
+    load_sem,
 ):
+    mask_load = pltpu.make_async_copy(mask_hbm, mask_ref, load_sem.at[0])
+    broken_load = pltpu.make_async_copy(broken_hbm, broken_ref, load_sem.at[1])
+    mask_load.start()
+    broken_load.start()
     slab, thick = axes
     si, ti = lax.axis_index(slab), lax.axis_index(thick)
     n_slab, n_thick = lax.axis_size(slab), lax.axis_size(thick)
@@ -225,6 +232,8 @@
     exchange(*payload)
     finish(*payload)
     tab[tiles:] = ghost_in[...]
+    mask_load.wait()
+    broken_load.wait()
 
     sub = lax.broadcasted_iota(jnp.int32, (8, 128), 0)
     cur_rows = (sub < 3).astype(f32)
@@ -391,9 +400,11 @@
             jax.ShapeDtypeStruct((3, tiles, 128), f32),
             jax.ShapeDtypeStruct((tiles, 128), f32),
         ),
-        in_specs=[smem] * 4 + [vmem] * 8,
+        in_specs=[smem] * 4 + [vmem] * 6 + [pl.BlockSpec(memory_space=pl.ANY)] * 2,
         out_specs=(vmem, vmem),
         scratch_shapes=[
+            pltpu.VMEM(bond_masks.shape, jnp.int32),
+            pltpu.VMEM(bond_masks.shape, jnp.int32),
             pltpu.VMEM((tiles + 12 * g, 8, 128), f32),
             pltpu.VMEM((4 * g, 8, 128), f32),
             pltpu.VMEM((12 * g, 8, 128), f32),
@@ -414,6 +425,7 @@
             pltpu.VMEM((12, g, 384), f32),
             pltpu.SemaphoreType.DMA((4, 12)),
             pltpu.SemaphoreType.DMA((4, 12)),
+            pltpu.SemaphoreType.DMA((2,)),
         ],
         compiler_params=pltpu.CompilerParams(
             collective_id=0, has_side_effects=True, vmem_limit_bytes=40 * 1024 * 1024

time: 88.1 us -> 78.2 us (0.89)
  Pallas kernels: 77.9 us -> 68.1 us
    pallas_call x1, Pallas kernels: 77.9 us -> 68.1 us  [body(): pl.pallas_call(functools.partial(kernel, ('slab', 'thick')), out_shape=(j...]
where the time goes in v2:
time: 78.2 us; the launch traced here: 77.4 us
  Pallas kernels  68.1 us (87%)
  local copies, waits for them, and re-layouts  8 us (10%)
  between operations  1.3 us (2%)
    pallas_call x1, Pallas kernels, body(): pl.pallas_call(functools.partial(kernel, ('slab', 'thick')), out_shape=(j...  68.1 us
    unnamed x18, local copies, waits for them, and re-layouts  7.92 us

profile of v2, /device:TPU:5, one launch (start us, length us, event | category | flops | bytes accessed | tf_op | source)
XLA Modules:
  0.0 77.4 jit_solution(4513271386068948075)
XLA Ops:
  1.3 0.0 copy-start.5
  1.3 0.7 copy-done.5
  2.0 0.0 copy-start.6
  2.0 0.0 copy-start.7
  2.0 0.1 reshape.24.list_vec
  2.0 0.6 copy-done.6
  2.6 0.0 copy-done.7
  2.6 0.0 copy-start
  2.6 1.2 %copy-done = s32[128,16,128]{2,1,0:T(8,128)S(1)} copy-done((s32[128,16,128]{2,1,0:T(8,128)S(1)}, s32[128,16,128]{2,1,0:T(8,128)}, u32[]{:S(2)}) %copy-start) | copy-done | bytes 1048600
  3.9 0.0 copy-start.1
  3.9 1.2 %copy-done.1 = s32[128,16,128]{2,1,0:T(8,128)S(1)} copy-done((s32[128,16,128]{2,1,0:T(8,128)S(1)}, s32[128,16,128]{2,1,0:T(8,128)}, u32[]{:S(2)}) %copy-start.1) | copy-done | bytes 1048600
  5.1 0.0 copy-start.2
  5.1 0.9 %copy-done.2 = f32[3,16384]{1,0:T(4,128)S(1)} copy-done((f32[3,16384]{1,0:T(4,128)S(1)}, f32[3,16384]{1,0:T(4,128)}, u32[]{:S(2)}) %copy-start.2) | copy-done | bytes 196632
  6.0 0.0 copy-start.3
  6.0 0.9 %copy-done.3 = f32[3,16384]{1,0:T(4,128)S(1)} copy-done((f32[3,16384]{1,0:T(4,128)S(1)}, f32[3,16384]{1,0:T(4,128)}, u32[]{:S(2)}) %copy-start.3) | copy-done | bytes 196632
  7.0 0.0 copy-start.4
  7.0 0.8 %copy-done.4 = f32[16384]{0:T(1024)S(1)} copy-done((f32[16384]{0:T(1024)S(1)}, f32[16384]{0:T(1024)}, u32[]{:S(2)}) %copy-start.4) | copy-done | bytes 65560
  7.8 68.1 %shard_map.104 = (f32[3,128,128]{2,1,0:T(8,128)S(1)}, f32[128,128]{1,0:T(8,128)S(1)}) custom-call(s32[128]{0:T(128)S(1)} %copy-done.6, s32[128]{0:T(128)S(1)} %copy-done.7, s32[1]{0:T(128)S(6)} %copy.15.count_ref, s32[2,2,16]{2,1,0:T(2,128)S(1)} %copy-done.5, s32[1,128]{1,0:T(1,128)S(1)} %bitcast.11, s32[1,128]{1,0:T(1,128)S(1)} %bitcast.12, ...), custom_call_target="tpu_custom_call" | custom-call | tf_op jit(solution)/shard_map/pallas_call | solution.py:397
  75.9 0.8 %copy.13 = f32[1,3,128,128]{3,1,2,0:T(4,128)} copy(f32[1,3,128,128]{3,2,1,0:T(8,128)S(1)} %bitcast.8) | data formatting | bytes 393216
  76.7 0.6 copy.16
Async XLA Ops:
  1.3 0.7 copy-start.5
  2.0 0.7 copy-start.6
  2.0 0.7 copy-start.7
  2.6 1.2 %copy-start = (s32[128,16,128]{2,1,0:T(8,128)S(1)}, s32[128,16,128]{2,1,0:T(8,128)}, u32[]{:S(2)}) copy-start(s32[128,16,128]{2,1,0:T(8,128)} %mask_hbm.1) | copy-start | bytes 3145732
  3.9 1.2 %copy-start.1 = (s32[128,16,128]{2,1,0:T(8,128)S(1)}, s32[128,16,128]{2,1,0:T(8,128)}, u32[]{:S(2)}) copy-start(s32[128,16,128]{2,1,0:T(8,128)} %broken_hbm.1) | copy-start | bytes 3145732
  5.1 0.9 %copy-start.2 = (f32[3,16384]{1,0:T(4,128)S(1)}, f32[3,16384]{1,0:T(4,128)}, u32[]{:S(2)}) copy-start(f32[3,16384]{1,0:T(4,128)} %pos_ref.1) | copy-start | bytes 589828
  6.0 0.9 %copy-start.3 = (f32[3,16384]{1,0:T(4,128)S(1)}, f32[3,16384]{1,0:T(4,128)}, u32[]{:S(2)}) copy-start(f32[3,16384]{1,0:T(4,128)} %disp_ref.1) | copy-start | bytes 589828
  7.0 0.8 %copy-start.4 = (f32[16384]{0:T(1024)S(1)}, f32[16384]{0:T(1024)}, u32[]{:S(2)}) copy-start(f32[16384]{0:T(1024)} %param.11) | copy-start | bytes 196612

commit v3 on v2

--- a/solution.py
+++ b/solution.py
@@ -99,13 +99,16 @@
     row_vec,
     col_vec,
     list_vec,
-    pos_ref,
-    disp_ref,
-    vol_ref,
+    pos_hbm,
+    disp_hbm,
+    vol_hbm,
     mask_hbm,
     broken_hbm,
     force_ref,
     dil_ref,
+    pos_ref,
+    disp_ref,
+    vol_ref,
     mask_ref,
     broken_ref,
     tab,
@@ -132,6 +135,13 @@
 ):
     mask_load = pltpu.make_async_copy(mask_hbm, mask_ref, load_sem.at[0])
     broken_load = pltpu.make_async_copy(broken_hbm, broken_ref, load_sem.at[1])
+    point_loads = [
+        pltpu.make_async_copy(pos_hbm, pos_ref, load_sem.at[2]),
+        pltpu.make_async_copy(disp_hbm, disp_ref, load_sem.at[3]),
+        pltpu.make_async_copy(vol_hbm, vol_ref, load_sem.at[4]),
+    ]
+    for load in point_loads:
+        load.start()
     mask_load.start()
     broken_load.start()
     slab, thick = axes
@@ -208,6 +218,8 @@
         )
         return carry
 
+    for load in point_loads:
+        load.wait()
     lax.fori_loop(0, tiles, build, 0, unroll=4)
 
     for s in range(2):
@@ -360,11 +372,11 @@
             col_force[c, pl.ds(k, 1), :] = cols[c : c + 1]
 
     def second_loop(block, carry):
-        for u in range(UNROLL):
-            second(block * UNROLL + u)
+        for u in range(2 * UNROLL):
+            second(block * 2 * UNROLL + u)
         return carry
 
-    lax.fori_loop(0, slots // UNROLL, second_loop, 0)
+    lax.fori_loop(0, slots // (2 * UNROLL), second_loop, 0)
 
     col_part = hot_dot(col_hot, jnp.concatenate([col_force[c] for c in range(3)], axis=1))
     force_out[...] = col_part[tiles:]
@@ -400,9 +412,12 @@
             jax.ShapeDtypeStruct((3, tiles, 128), f32),
             jax.ShapeDtypeStruct((tiles, 128), f32),
         ),
-        in_specs=[smem] * 4 + [vmem] * 6 + [pl.BlockSpec(memory_space=pl.ANY)] * 2,
+        in_specs=[smem] * 4 + [vmem] * 3 + [pl.BlockSpec(memory_space=pltpu.HBM)] * 5,
         out_specs=(vmem, vmem),
         scratch_shapes=[
+            pltpu.VMEM(ref_pos.shape, f32),
+            pltpu.VMEM(displacement.shape, f32),
+            pltpu.VMEM((tiles, 128), f32),
             pltpu.VMEM(bond_masks.shape, jnp.int32),
             pltpu.VMEM(bond_masks.shape, jnp.int32),
             pltpu.VMEM((tiles + 12 * g, 8, 128), f32),
@@ -425,7 +440,7 @@
             pltpu.VMEM((12, g, 384), f32),
             pltpu.SemaphoreType.DMA((4, 12)),
             pltpu.SemaphoreType.DMA((4, 12)),
-            pltpu.SemaphoreType.DMA((2,)),
+            pltpu.SemaphoreType.DMA((5,)),
         ],
         compiler_params=pltpu.CompilerParams(
             collective_id=0, has_side_effects=True, vmem_limit_bytes=40 * 1024 * 1024

time: 78.2 us -> 76.4 us (0.977)
  Pallas kernels: 68.1 us -> 66.2 us
    pallas_call x1, Pallas kernels: 68.1 us -> 66.2 us  [body(): pl.pallas_call(functools.partial(kernel, ('slab', 'thick')), out_shape=(j...]
where the time goes in v3:
time: 76.4 us; the launch traced here: 75.5 us
  Pallas kernels  66.2 us (87%)
  local copies, waits for them, and re-layouts  8 us (10%)
  between operations  1.3 us (2%)
    pallas_call x1, Pallas kernels, body(): pl.pallas_call(functools.partial(kernel, ('slab', 'thick')), out_shape=(j...  66.2 us
    unnamed x18, local copies, waits for them, and re-layouts  7.92 us

profile of v3, /device:TPU:5, one launch (start us, length us, event | category | flops | bytes accessed | tf_op | source)
XLA Modules:
  0.0 75.5 jit_solution(14481065941347265694)
XLA Ops:
  1.3 0.0 copy-start.5
  1.3 0.7 copy-done.5
  2.0 0.0 copy-start.6
  2.0 0.0 copy-start.7
  2.0 0.1 reshape.24.list_vec
  2.0 0.6 copy-done.6
  2.6 0.0 copy-done.7
  2.6 0.0 copy-start
  2.6 1.2 %copy-done = s32[128,16,128]{2,1,0:T(8,128)S(1)} copy-done((s32[128,16,128]{2,1,0:T(8,128)S(1)}, s32[128,16,128]{2,1,0:T(8,128)}, u32[]{:S(2)}) %copy-start) | copy-done | bytes 1048600
  3.9 0.0 copy-start.1
  3.9 1.2 %copy-done.1 = s32[128,16,128]{2,1,0:T(8,128)S(1)} copy-done((s32[128,16,128]{2,1,0:T(8,128)S(1)}, s32[128,16,128]{2,1,0:T(8,128)}, u32[]{:S(2)}) %copy-start.1) | copy-done | bytes 1048600
  5.1 0.0 copy-start.2
  5.1 0.9 %copy-done.2 = f32[3,16384]{1,0:T(4,128)S(1)} copy-done((f32[3,16384]{1,0:T(4,128)S(1)}, f32[3,16384]{1,0:T(4,128)}, u32[]{:S(2)}) %copy-start.2) | copy-done | bytes 196632
  6.0 0.0 copy-start.3
  6.0 0.9 %copy-done.3 = f32[3,16384]{1,0:T(4,128)S(1)} copy-done((f32[3,16384]{1,0:T(4,128)S(1)}, f32[3,16384]{1,0:T(4,128)}, u32[]{:S(2)}) %copy-start.3) | copy-done | bytes 196632
  7.0 0.0 copy-start.4
  7.0 0.8 %copy-done.4 = f32[16384]{0:T(1024)S(1)} copy-done((f32[16384]{0:T(1024)S(1)}, f32[16384]{0:T(1024)}, u32[]{:S(2)}) %copy-start.4) | copy-done | bytes 65560
  7.8 66.2 %shard_map.104 = (f32[3,128,128]{2,1,0:T(8,128)S(1)}, f32[128,128]{1,0:T(8,128)S(1)}) custom-call(s32[128]{0:T(128)S(1)} %copy-done.6, s32[128]{0:T(128)S(1)} %copy-done.7, s32[1]{0:T(128)S(6)} %copy.15.count_ref, s32[2,2,16]{2,1,0:T(2,128)S(1)} %copy-done.5, s32[1,128]{1,0:T(1,128)S(1)} %bitcast.11, s32[1,128]{1,0:T(1,128)S(1)} %bitcast.12, ...), custom_call_target="tpu_custom_call" | custom-call | tf_op jit(solution)/shard_map/pallas_call | solution.py:409
  74.0 0.8 %copy.13 = f32[1,3,128,128]{3,1,2,0:T(4,128)} copy(f32[1,3,128,128]{3,2,1,0:T(8,128)S(1)} %bitcast.8) | data formatting | bytes 393216
  74.9 0.6 copy.16
Async XLA Ops:
  1.3 0.7 copy-start.5
  2.0 0.7 copy-start.6
  2.0 0.7 copy-start.7
  2.6 1.2 %copy-start = (s32[128,16,128]{2,1,0:T(8,128)S(1)}, s32[128,16,128]{2,1,0:T(8,128)}, u32[]{:S(2)}) copy-start(s32[128,16,128]{2,1,0:T(8,128)} %mask_hbm.1) | copy-start | bytes 3145732
  3.9 1.2 %copy-start.1 = (s32[128,16,128]{2,1,0:T(8,128)S(1)}, s32[128,16,128]{2,1,0:T(8,128)}, u32[]{:S(2)}) copy-start(s32[128,16,128]{2,1,0:T(8,128)} %broken_hbm.1) | copy-start | bytes 3145732
  5.1 0.9 %copy-start.2 = (f32[3,16384]{1,0:T(4,128)S(1)}, f32[3,16384]{1,0:T(4,128)}, u32[]{:S(2)}) copy-start(f32[3,16384]{1,0:T(4,128)} %pos_hbm.1) | copy-start | bytes 589828
  6.0 0.9 %copy-start.3 = (f32[3,16384]{1,0:T(4,128)S(1)}, f32[3,16384]{1,0:T(4,128)}, u32[]{:S(2)}) copy-start(f32[3,16384]{1,0:T(4,128)} %disp_hbm.1) | copy-start | bytes 589828
  7.0 0.8 %copy-start.4 = (f32[16384]{0:T(1024)S(1)}, f32[16384]{0:T(1024)}, u32[]{:S(2)}) copy-start(f32[16384]{0:T(1024)} %param.11) | copy-start | bytes 196612
